TPU v7x, 32 devices: a whole 2x2x4 slice. The times are simulated.
32 devices in a mesh: groups: 2 (over y), row: 4 (over z), col: 4 (over x, core).
Axes of the slice: x: 2, y: 2, z: 4, core: 2. Of those that a mesh axis runs over, the one named last changes fastest.
Arguments:
- positions: float32 [3, 2048], P(None, ('groups', 'row', 'col')), parts along dimension 1, as said below
- probes: float32 [3, 16, 2048], P(None, None, ('groups', 'row', 'col')), parts along dimension 2, may hold values from -6 to 6
Outputs:
- noise_field: float32 [3, 16, 2048], P(None, None, ('groups', 'row', 'col')), parts along dimension 2
There are 2 independent parts, one for each index of `groups`. A program takes and returns all parts, laid end to end along the dimension named above; each array names one. Nothing has to cross between parts.
Inputs may be any that keep to these rules, and one draw needn't show every extreme that they name: `positions`: beads lie near the points of a lattice of unit spacing, 16 by 16 by 4 layers, bead i near (i % 16, (i // 16) % 16, i // 256), each coordinate within 0.2 of it, so that no two beads are closer than 2 a.
All inputs are finite; a program needn't handle non-finite values.
Results may differ from a plain program's by a relative error of at most 0.0003.
Values sent between devices are 32-bit elements; how exact they have to be, the bound alone decides.
A program may use at most 128 MiB of HBM per device.

v0:
```python
import functools
import math

import jax
import jax.numpy as jnp
from jax import lax
from jax.experimental import pallas as pl
from jax.experimental.pallas import tpu as pltpu
from jax.sharding import PartitionSpec as P

DEG = 4
RADIUS = 0.3
MESH = pl.DeviceIdType.MESH
F32 = jnp.float32
BF16 = jnp.bfloat16


def cheb_weight(degree_step):
    if degree_step == 0:
        return 2.0 / math.pi
    return 4.0 * (-1.0) ** (degree_step + 1) / (math.pi * (4.0 * degree_step * degree_step - 1.0))


def flip(index, bits):
    for bit in (1, 2, 4, 8):
        if bits & bit:
            index = index + bit - 2 * bit * lax.rem(lax.div(index, bit), 2)
    return index


def split(value):
    high = value.astype(BF16)
    return high, (value - high.astype(F32)).astype(BF16)


def kernel(
    pos_hbm, probes_hbm, out_ref,
    pos_ref, probes_ref, msg, first, field, posT, w_high, w_low, gather, last_out, last_in,
    load, first_send, first_recv, gather_send, gather_recv, last_send, last_recv,
):
    row = lax.axis_index("row")
    col = lax.axis_index("col")
    partners = [(dr, dc) for dc in range(4) for dr in (2, 3, 1, 0) if (dr, dc) != (0, 0)]

    loads = [
        pltpu.make_async_copy(pos_hbm, pos_ref, load.at[0]),
        pltpu.make_async_copy(probes_hbm, probes_ref, load.at[1]),
    ]
    for copy in loads:
        copy.start()
    barrier = pltpu.get_barrier_semaphore()
    for dr, dc in partners:
        pl.semaphore_signal(
            barrier, inc=1, device_id={"row": flip(row, dr), "col": flip(col, dc)}, device_id_type=MESH
        )
    for copy in loads:
        copy.wait()

    scaled_pos = pos_ref[...] * (1.0 / (0.75 * RADIUS))
    for r in range(4):
        mine = [probes_ref[t, 4 * r : 4 * r + 4, :] for t in range(3)]
        left = jnp.concatenate([mine[0], mine[1]], axis=0)
        right = jnp.concatenate([mine[2], scaled_pos, jnp.zeros((1, 64), F32)], axis=0)
        msg[r] = jnp.concatenate([left, right], axis=1)
    first[0, 0] = msg[row]

    pl.semaphore_wait(barrier, len(partners))
    first_copies = {}
    for dr, dc in partners:
        to_row = flip(row, dr)
        copy = pltpu.make_async_remote_copy(
            src_ref=msg.at[to_row],
            dst_ref=first.at[dc, dr],
            send_sem=first_send.at[dc, dr],
            recv_sem=first_recv.at[dc, dr],
            device_id={"row": to_row, "col": flip(col, dc)},
            device_id_type=MESH,
        )
        copy.start()
        first_copies[dc, dr] = copy

    low_lanes = lax.broadcasted_iota(jnp.int32, (8, 128), 1) < 64

    def unpack(dc):
        for h in range(2):
            even, odd = first[dc, 2 * h], first[dc, 2 * h + 1]
            lanes = slice(128 * h, 128 * h + 128)
            field[dc, 0:8, lanes] = jnp.where(low_lanes, even, pltpu.roll(odd, 64, 1))
            field[dc, 8:16, lanes] = jnp.where(low_lanes, pltpu.roll(even, 64, 1), odd)
        pair = jnp.concatenate([field[dc, 8:16, 0:128], field[dc, 8:16, 128:256]], axis=0)
        posT[dc] = pair.T

    unit = (0.75 * RADIUS) ** 2
    c_along = 2.0 / 3.0 * RADIUS * RADIUS / unit
    c_across = 2.0 * RADIUS * RADIUS / unit
    STEP = 16
    own_bead = lax.broadcasted_iota(jnp.int32, (STEP, 128), 1)
    step_bead = lax.broadcasted_iota(jnp.int32, (STEP, 128), 0)
    sums = [[jnp.zeros((8, 128), F32) for _ in range(3)] for _ in range(2)]

    def generate(dc, h):
        for at in range(0, 128, STEP):
            rows = slice(256 * dc + 128 * h + at, 256 * dc + 128 * h + at + STEP)
            centres = [posT[dc, at : at + STEP, 8 * h + 4 + t : 8 * h + 5 + t] for t in range(3)]
            centres = [jnp.broadcast_to(c, (STEP, 128)) for c in centres]
            for own in range(2):
                d = [field[0, 12 + t : 13 + t, 128 * own : 128 * own + 128] - centres[t] for t in range(3)]
                dist_sq = d[0] * d[0] + d[1] * d[1] + d[2] * d[2]
                diagonal = dc == 0 and own == h
                if diagonal:
                    same = (step_bead + at) == own_bead
                    dist_sq = jnp.where(same, 1.0, dist_sq)
                inverse = lax.rsqrt(dist_sq)
                inv_sq = inverse * inverse
                cubed = inverse * inv_sq
                along = inverse + c_along * cubed
                across = cubed - c_across * (cubed * inv_sq)
                if diagonal:
                    along = jnp.where(same, 1.0, along)
                    across = jnp.where(same, 0.0, across)
                g = [across * d[t] for t in range(3)]
                parts = [
                    along + g[0] * d[0], along + g[1] * d[1], along + g[2] * d[2],
                    g[0] * d[1], g[0] * d[2], g[1] * d[2],
                ]
                for k, part in enumerate(parts):
                    high, low = split(part)
                    lanes = slice(768 * own + 128 * k, 768 * own + 128 * k + 128)
                    w_high[rows, lanes] = high
                    w_low[rows, lanes] = low
                mags = [jnp.abs(part) for part in parts]
                mags = [mag[0:8] + mag[8:16] for mag in mags]
                for t, (p, q, r) in enumerate(((0, 3, 4), (1, 3, 5), (2, 4, 5))):
                    sums[own][t] = sums[own][t] + (mags[p] + mags[q] + mags[r])

    def multiply(blocks, dc):
        rows = slice(256 * dc, 256 * (dc + len(blocks)))
        high, low = split(jnp.concatenate(blocks, axis=1))
        both = jnp.concatenate([high, low], axis=0)
        image = jnp.dot(both, w_high[rows], preferred_element_type=F32)
        rest = jnp.dot(high, w_low[rows], preferred_element_type=F32)
        return image[0:16] + image[16:32] + rest

    def combine(acc):
        halves = []
        for own in range(2):
            xx, yy, zz, xy, xz, yz = [
                acc[:, 768 * own + 128 * k : 768 * own + 128 * k + 128] for k in range(6)
            ]
            halves.append(
                jnp.concatenate(
                    [
                        xx[0:4] + xy[4:8] + xz[8:12],
                        xy[0:4] + yy[4:8] + yz[8:12],
                        xz[0:4] + yz[4:8] + zz[8:12],
                    ],
                    axis=0,
                )
            )
        return jnp.concatenate(halves, axis=1)

    def send(k, value):
        gather[k, 0] = value
        copies = {}
        for dc in (3, 2, 1):
            copy = pltpu.make_async_remote_copy(
                src_ref=gather.at[k, 0],
                dst_ref=gather.at[k, dc],
                send_sem=gather_send.at[k, dc],
                recv_sem=gather_recv.at[k, dc],
                device_id={"row": row, "col": flip(col, dc)},
                device_id_type=MESH,
            )
            copy.start()
            copies[dc] = copy
        return copies

    def apply(k, copies):
        acc = multiply([gather[k, 0]], 0)
        for dc in range(1, 4):
            copies[dc].wait_recv()
        return combine(acc + multiply([gather[k, dc] for dc in range(1, 4)], 1))

    for dr in (2, 3, 1):
        first_copies[0, dr].wait_recv()
    unpack(0)
    generate(0, 0)
    generate(0, 1)
    for dc in range(1, 4):
        for dr in range(4):
            first_copies[dc, dr].wait_recv()
    for dc in range(1, 4):
        unpack(dc)
    acc = None
    for dc in range(1, 4):
        generate(dc, 0)
        term = multiply([field[dc - 1]], dc - 1)
        acc = term if acc is None else acc + term
        generate(dc, 1)
    acc = acc + multiply([field[3]], 3)
    image1 = combine(acc)
    row_max = functools.reduce(jnp.maximum, [jnp.sum(s, axis=0, keepdims=True) for half in sums for s in half])
    row_max = jnp.max(row_max, axis=1, keepdims=True)
    copies1 = send(0, jnp.concatenate([image1, jnp.broadcast_to(row_max, (4, 256))], axis=0))
    image2 = apply(0, copies1)
    top = functools.reduce(jnp.maximum, [gather[0, dc, 12:13, :] for dc in range(4)])
    factor = 2.0 / top
    start = field[0, 0:12, :]
    basis1 = factor * image1 - start
    basis2 = 2.0 * (factor * (factor * image2 - image1) - basis1) - start
    pad = jnp.zeros((4, 256), F32)
    copies2 = send(1, jnp.concatenate([basis2, pad], axis=0))
    basis3 = 2.0 * (factor * apply(1, copies2) - basis2) - basis1
    copies3 = send(2, jnp.concatenate([basis3, pad], axis=0))
    noise = cheb_weight(0) * start + cheb_weight(1) * basis1
    noise = noise + cheb_weight(2) * basis2 + cheb_weight(3) * basis3
    basis4 = 2.0 * (factor * apply(2, copies3) - basis3) - basis2
    noise = jnp.sqrt(top) * (noise + cheb_weight(4) * basis4)

    noise = jnp.concatenate([noise, pad], axis=0)
    last_copies = []
    for dr in (2, 3, 1, 0):
        h = dr // 2
        upper = noise[0:8, 128 * h : 128 * h + 128]
        lower = noise[8:16, 128 * h : 128 * h + 128]
        if dr % 2 == 0:
            tile = jnp.where(low_lanes, upper, pltpu.roll(lower, 64, 1))
        else:
            tile = jnp.where(low_lanes, pltpu.roll(upper, 64, 1), lower)
        if dr == 0:
            last_in[row] = tile
        else:
            last_out[dr] = tile
            copy = pltpu.make_async_remote_copy(
                src_ref=last_out.at[dr],
                dst_ref=last_in.at[row],
                send_sem=last_send.at[dr],
                recv_sem=last_recv.at[dr],
                device_id={"row": flip(row, dr), "col": col},
                device_id_type=MESH,
            )
            copy.start()
            last_copies.append(copy)
    for copy in list(first_copies.values()):
        copy.wait_send()
    for copies in (copies1, copies2, copies3):
        for copy in copies.values():
            copy.wait_send()
    for copy in last_copies:
        copy.wait()
    for q in range(4):
        tile = last_in[q]
        out_ref[0, 4 * q : 4 * q + 4, :] = tile[0:4, 0:64]
        out_ref[1, 4 * q : 4 * q + 4, :] = tile[4:8, 0:64]
        out_ref[2, 4 * q : 4 * q + 4, :] = tile[0:4, 64:128]


def fused(positions, probes):
    DMA = pltpu.SemaphoreType.DMA
    return pl.pallas_call(
        kernel,
        out_shape=jax.ShapeDtypeStruct(probes.shape, F32),
        in_specs=[pl.BlockSpec(memory_space=pltpu.HBM)] * 2,
        out_specs=pl.BlockSpec(memory_space=pltpu.VMEM),
        scratch_shapes=[
            pltpu.VMEM(positions.shape, F32),
            pltpu.VMEM(probes.shape, F32),
            pltpu.VMEM((4, 8, 128), F32),
            pltpu.VMEM((4, 4, 8, 128), F32),
            pltpu.VMEM((4, 16, 256), F32),
            pltpu.VMEM((4, 128, 16), F32),
            pltpu.VMEM((1024, 1536), BF16),
            pltpu.VMEM((1024, 1536), BF16),
            pltpu.VMEM((DEG - 1, 4, 16, 256), F32),
            pltpu.VMEM((4, 8, 128), F32),
            pltpu.VMEM((4, 8, 128), F32),
            DMA((2,)),
            DMA((4, 4)),
            DMA((4, 4)),
            DMA((DEG - 1, 4)),
            DMA((DEG - 1, 4)),
            DMA((4,)),
            DMA((4,)),
        ],
        compiler_params=pltpu.CompilerParams(
            collective_id=0, has_side_effects=True, vmem_limit_bytes=32 * 1024 * 1024
        ),
        name="fused",
    )(*[pltpu.with_memory_space_constraint(x, pltpu.HBM) for x in (positions, probes)])


def block_width(length):
    width = min(length, 512)
    while length % width != 0:
        width = width - 1
    return width


def mobility_block(rows_pos, rows_ids, cols_pos, cols_ids):
    delta = rows_pos[:, :, None] - cols_pos[:, None, :]
    dist_sq = jnp.sum(delta * delta, axis=0)
    same = rows_ids[:, None] == cols_ids[None, :]
    inverse = lax.rsqrt(dist_sq + same.astype(jnp.float32))
    inv_sq = inverse * inverse
    scaled = 0.75 * RADIUS * inverse
    along = jnp.where(same, jnp.float32(1.0), scaled * (1.0 + 2.0 / 3.0 * RADIUS * RADIUS * inv_sq))
    across = jnp.where(
        same, jnp.float32(0.0), scaled * inv_sq * (1.0 - 2.0 * RADIUS * RADIUS * inv_sq)
    )
    identity = jnp.eye(3, dtype=jnp.float32)
    return (
        identity[:, :, None, None] * along[None, None]
        + delta[:, None] * (across[None] * delta)[None]
    )


def gathered(positions, probes):
    seg_len = positions.shape[1]
    probe_count = probes.shape[1]
    n_row = lax.axis_size("row")
    n_col = lax.axis_size("col")
    beads_all = seg_len * n_row * n_col
    places = lax.all_gather(positions, ("row", "col"), axis=1, tiled=True)
    all_ids = jnp.arange(beads_all, dtype=jnp.int32)
    own_at = (lax.axis_index("row") * n_col + lax.axis_index("col")) * seg_len
    own_ids = own_at + jnp.arange(seg_len, dtype=jnp.int32)
    width = block_width(beads_all)

    def apply_mobility(vectors):
        whole = lax.all_gather(vectors, ("row", "col"), axis=2, tiled=True)

        def add_block(block_step, carried):
            offset = block_step * width
            cols_pos = lax.dynamic_slice_in_dim(places, offset, width, 1)
            cols_ids = lax.dynamic_slice_in_dim(all_ids, offset, width, 0)
            mobility = mobility_block(positions, own_ids, cols_pos, cols_ids)
            columns = lax.dynamic_slice_in_dim(whole, offset, width, 2)
            image = carried[0] + jnp.einsum(
                "abrc,bpc->apr", mobility, columns, precision=lax.Precision.HIGHEST
            )
            return image, carried[1] + jnp.sum(jnp.abs(mobility), axis=(1, 3))

        zeros = (jnp.zeros((3, probe_count, seg_len), F32), jnp.zeros((3, seg_len), F32))
        return lax.fori_loop(0, beads_all // width, add_block, zeros)

    image, row_sums = apply_mobility(probes)
    ceiling = lax.pmax(jnp.max(row_sums), ("row", "col"))
    factor = 2.0 / ceiling
    previous = probes
    current = factor * image - probes
    noise_sum = cheb_weight(0) * previous + cheb_weight(1) * current
    for degree_step in range(2, DEG + 1):
        following = 2.0 * (factor * apply_mobility(current)[0] - current) - previous
        previous, current = (current, following)
        noise_sum = noise_sum + cheb_weight(degree_step) * current
    return jnp.sqrt(ceiling) * noise_sum


def solution(mesh):
    split_by = ("groups", "row", "col")
    square = mesh.shape["row"] == 4 and mesh.shape["col"] == 4

    def per_device(positions, probes):
        if square and probes.shape == (3, 16, 64):
            return fused(positions, probes)
        return gathered(positions, probes)

    return jax.shard_map(
        per_device,
        mesh=mesh,
        in_specs=(P(None, split_by), P(None, None, split_by)),
        out_specs=P(None, None, split_by),
        check_vma=False,
    )
```

profile of v0, /device:TPU:0, one launch (start us, length us, event | category | flops | bytes accessed | tf_op | source)
XLA Modules:
  0.0 29.0 jit_solution(11537749264936058692)
XLA Ops:
  0.0 28.4 %fused.1 = f32[3,16,64]{2,1,0:T(8,128)S(1)} custom-call(f32[3,64]{1,0:T(4,128)} %pos_hbm.1, f32[3,16,64]{2,1,0:T(8,128)} %probes_hbm.1), custom_call_target="tpu_custom_call" | custom-call | tf_op jit(solution)/shard_map/fused/pallas_call | solution.py:260
  28.4 0.6 %copy.4 = f32[3,16,64]{2,1,0:T(8,128)} copy(f32[3,16,64]{2,1,0:T(8,128)S(1)} %fused.1) | data formatting | bytes 24576
where the time goes:
time: 29.2 us; the launch traced here: 29 us
  Pallas kernels  28.4 us (97%)
  local copies, waits for them, and re-layouts  0.61 us (2%)
    pallas_call x1, Pallas kernels, fused(): pl.pallas_call(kernel, out_shape=jax.ShapeDtypeStruct(probes.shape, F32),...  28.4 us
    unnamed x1, local copies, waits for them, and re-layouts  0.61 us

commit v1 on v0

--- a/solution.py
+++ b/solution.py
@@ -35,7 +35,7 @@
 
 def kernel(
     pos_hbm, probes_hbm, out_ref,
-    pos_ref, probes_ref, msg, first, field, posT, w_high, w_low, gather, last_out, last_in,
+    pos_ref, probes_ref, msg, first, field, posT, w_high, w_low, gather, states, last_out, last_in,
     load, first_send, first_recv, gather_send, gather_recv, last_send, last_recv,
 ):
     row = lax.axis_index("row")
@@ -60,7 +60,7 @@
     for r in range(4):
         mine = [probes_ref[t, 4 * r : 4 * r + 4, :] for t in range(3)]
         left = jnp.concatenate([mine[0], mine[1]], axis=0)
-        right = jnp.concatenate([mine[2], scaled_pos, jnp.zeros((1, 64), F32)], axis=0)
+        right = jnp.concatenate([mine[2], scaled_pos, jnp.ones((1, 64), F32)], axis=0)
         msg[r] = jnp.concatenate([left, right], axis=1)
     first[0, 0] = msg[row]
 
@@ -96,17 +96,18 @@
     STEP = 16
     own_bead = lax.broadcasted_iota(jnp.int32, (STEP, 128), 1)
     step_bead = lax.broadcasted_iota(jnp.int32, (STEP, 128), 0)
-    sums = [[jnp.zeros((8, 128), F32) for _ in range(3)] for _ in range(2)]
-
-    def generate(dc, h):
+
+    def generate(dc, h, sums):
+        sums = [list(half) for half in sums]
         for at in range(0, 128, STEP):
-            rows = slice(256 * dc + 128 * h + at, 256 * dc + 128 * h + at + STEP)
-            centres = [posT[dc, at : at + STEP, 8 * h + 4 + t : 8 * h + 5 + t] for t in range(3)]
+            rows = pl.ds(pl.multiple_of(256 * dc + 128 * h + at, STEP), STEP)
+            centres = posT[dc, at : at + STEP, :]
+            centres = [centres[:, 8 * h + 4 + t : 8 * h + 5 + t] for t in range(3)]
             centres = [jnp.broadcast_to(c, (STEP, 128)) for c in centres]
             for own in range(2):
                 d = [field[0, 12 + t : 13 + t, 128 * own : 128 * own + 128] - centres[t] for t in range(3)]
                 dist_sq = d[0] * d[0] + d[1] * d[1] + d[2] * d[2]
-                diagonal = dc == 0 and own == h
+                diagonal = isinstance(dc, int) and dc == 0 and own == h
                 if diagonal:
                     same = (step_bead + at) == own_bead
                     dist_sq = jnp.where(same, 1.0, dist_sq)
@@ -128,17 +129,17 @@
                     lanes = slice(768 * own + 128 * k, 768 * own + 128 * k + 128)
                     w_high[rows, lanes] = high
                     w_low[rows, lanes] = low
-                mags = [jnp.abs(part) for part in parts]
-                mags = [mag[0:8] + mag[8:16] for mag in mags]
-                for t, (p, q, r) in enumerate(((0, 3, 4), (1, 3, 5), (2, 4, 5))):
-                    sums[own][t] = sums[own][t] + (mags[p] + mags[q] + mags[r])
-
-    def multiply(blocks, dc):
-        rows = slice(256 * dc, 256 * (dc + len(blocks)))
-        high, low = split(jnp.concatenate(blocks, axis=1))
+                for t in range(3):
+                    mag = jnp.abs(parts[3 + t])
+                    sums[own][t] = sums[own][t] + (mag[0:8] + mag[8:16])
+        return tuple(tuple(half) for half in sums)
+
+    def multiply(block, dc):
+        rows = pl.ds(pl.multiple_of(256 * dc, 256), 256)
+        high, low = split(block)
         both = jnp.concatenate([high, low], axis=0)
-        image = jnp.dot(both, w_high[rows], preferred_element_type=F32)
-        rest = jnp.dot(high, w_low[rows], preferred_element_type=F32)
+        image = jnp.dot(both, w_high[rows, :], preferred_element_type=F32)
+        rest = jnp.dot(high, w_low[rows, :], preferred_element_type=F32)
         return image[0:16] + image[16:32] + rest
 
     def combine(acc):
@@ -159,63 +160,86 @@
             )
         return jnp.concatenate(halves, axis=1)
 
+    def gather_copy(k, dc, to_col):
+        return pltpu.make_async_remote_copy(
+            src_ref=gather.at[k, 0],
+            dst_ref=gather.at[k, dc],
+            send_sem=gather_send.at[k, dc],
+            recv_sem=gather_recv.at[k, dc],
+            device_id={"row": row, "col": to_col},
+            device_id_type=MESH,
+        )
+
     def send(k, value):
         gather[k, 0] = value
-        copies = {}
         for dc in (3, 2, 1):
-            copy = pltpu.make_async_remote_copy(
-                src_ref=gather.at[k, 0],
-                dst_ref=gather.at[k, dc],
-                send_sem=gather_send.at[k, dc],
-                recv_sem=gather_recv.at[k, dc],
-                device_id={"row": row, "col": flip(col, dc)},
-                device_id_type=MESH,
-            )
-            copy.start()
-            copies[dc] = copy
-        return copies
-
-    def apply(k, copies):
-        acc = multiply([gather[k, 0]], 0)
-        for dc in range(1, 4):
-            copies[dc].wait_recv()
-        return combine(acc + multiply([gather[k, dc] for dc in range(1, 4)], 1))
+            gather_copy(k, dc, flip(col, dc)).start()
 
     for dr in (2, 3, 1):
         first_copies[0, dr].wait_recv()
     unpack(0)
-    generate(0, 0)
-    generate(0, 1)
+    sums = tuple(tuple(jnp.zeros((8, 128), F32) for _ in range(3)) for _ in range(2))
+    sums = generate(0, 0, sums)
+    sums = generate(0, 1, sums)
     for dc in range(1, 4):
         for dr in range(4):
             first_copies[dc, dr].wait_recv()
     for dc in range(1, 4):
         unpack(dc)
-    acc = None
-    for dc in range(1, 4):
-        generate(dc, 0)
-        term = multiply([field[dc - 1]], dc - 1)
-        acc = term if acc is None else acc + term
-        generate(dc, 1)
-    acc = acc + multiply([field[3]], 3)
+
+    def grow(dc, carried):
+        acc, sums = carried
+        sums = generate(dc, 0, sums)
+        acc = acc + multiply(field[dc - 1], dc - 1)
+        return acc, generate(dc, 1, sums)
+
+    acc, sums = lax.fori_loop(1, 4, grow, (jnp.zeros((16, 1536), F32), sums))
+    acc = acc + multiply(field[3], 3)
     image1 = combine(acc)
-    row_max = functools.reduce(jnp.maximum, [jnp.sum(s, axis=0, keepdims=True) for half in sums for s in half])
+    row_max = None
+    for own in range(2):
+        xx, yy, zz = [acc[15:16, 768 * own + 128 * k : 768 * own + 128 * k + 128] for k in range(3)]
+        xy, xz, yz = [jnp.sum(s, axis=0, keepdims=True) for s in sums[own]]
+        largest = jnp.maximum(jnp.maximum(xx + xy + xz, xy + yy + yz), xz + yz + zz)
+        row_max = largest if row_max is None else jnp.maximum(row_max, largest)
     row_max = jnp.max(row_max, axis=1, keepdims=True)
-    copies1 = send(0, jnp.concatenate([image1, jnp.broadcast_to(row_max, (4, 256))], axis=0))
-    image2 = apply(0, copies1)
+    send(0, jnp.concatenate([image1, jnp.broadcast_to(row_max, (4, 256))], axis=0))
+
+    pad = jnp.zeros((4, 256), F32)
+    states[0, 0:12] = field[0, 0:12, :]
+    states[1, 0:12] = image1
+
+    def degree(k, carried):
+        def block(dc, acc):
+            @pl.when(dc > 0)
+            def _():
+                gather_copy(k, dc, flip(col, 1)).wait_recv()
+
+            return acc + multiply(gather[k, dc], dc)
+
+        image = combine(lax.fori_loop(0, 4, block, jnp.zeros((16, 1536), F32)))
+        top = functools.reduce(jnp.maximum, [gather[0, dc, 12:13, :] for dc in range(4)])
+        factor = 2.0 / top
+        older, last = states[0, 0:12], states[1, 0:12]
+        opening = k == 0
+        last1 = jnp.where(opening, factor * last - older, last)
+        image = factor * jnp.where(opening, factor * image - last, image)
+        following = 2.0 * (image - last1) - older
+        total = jnp.where(opening, cheb_weight(0) * older + cheb_weight(1) * last1, states[2, 0:12])
+        weight = jnp.where(opening, cheb_weight(2), jnp.where(k == 1, cheb_weight(3), cheb_weight(4)))
+        states[2, 0:12] = total + weight * following
+        states[0, 0:12] = last1
+        states[1, 0:12] = following
+
+        @pl.when(k < DEG - 2)
+        def _():
+            send(k + 1, jnp.concatenate([following, pad], axis=0))
+
+        return carried
+
+    lax.fori_loop(0, DEG - 1, degree, 0)
     top = functools.reduce(jnp.maximum, [gather[0, dc, 12:13, :] for dc in range(4)])
-    factor = 2.0 / top
-    start = field[0, 0:12, :]
-    basis1 = factor * image1 - start
-    basis2 = 2.0 * (factor * (factor * image2 - image1) - basis1) - start
-    pad = jnp.zeros((4, 256), F32)
-    copies2 = send(1, jnp.concatenate([basis2, pad], axis=0))
-    basis3 = 2.0 * (factor * apply(1, copies2) - basis2) - basis1
-    copies3 = send(2, jnp.concatenate([basis3, pad], axis=0))
-    noise = cheb_weight(0) * start + cheb_weight(1) * basis1
-    noise = noise + cheb_weight(2) * basis2 + cheb_weight(3) * basis3
-    basis4 = 2.0 * (factor * apply(2, copies3) - basis3) - basis2
-    noise = jnp.sqrt(top) * (noise + cheb_weight(4) * basis4)
+    noise = jnp.sqrt(top) * states[2, 0:12]
 
     noise = jnp.concatenate([noise, pad], axis=0)
     last_copies = []
@@ -243,9 +267,9 @@
             last_copies.append(copy)
     for copy in list(first_copies.values()):
         copy.wait_send()
-    for copies in (copies1, copies2, copies3):
-        for copy in copies.values():
-            copy.wait_send()
+    for k in range(DEG - 1):
+        for dc in (3, 2, 1):
+            gather_copy(k, dc, flip(col, dc)).wait_send()
     for copy in last_copies:
         copy.wait()
     for q in range(4):
@@ -272,6 +296,7 @@
             pltpu.VMEM((1024, 1536), BF16),
             pltpu.VMEM((1024, 1536), BF16),
             pltpu.VMEM((DEG - 1, 4, 16, 256), F32),
+            pltpu.VMEM((3, 16, 256), F32),
             pltpu.VMEM((4, 8, 128), F32),
             pltpu.VMEM((4, 8, 128), F32),
             DMA((2,)),

time: 29.2 us -> 29.4 us (level)
  no operation moved by 1% of the time
where the time goes in v1:
time: 29.4 us; the launch traced here: 29.2 us
  Pallas kernels  28.6 us (97%)
  local copies, waits for them, and re-layouts  0.61 us (2%)
    pallas_call x1, Pallas kernels, fused(): pl.pallas_call(kernel, out_shape=jax.ShapeDtypeStruct(probes.shape, F32),...  28.6 us
    unnamed x1, local copies, waits for them, and re-layouts  0.61 us

profile of v1, /device:TPU:0, one launch (start us, length us, event | category | flops | bytes accessed | tf_op | source)
XLA Modules:
  0.0 29.2 jit_solution(8156586671327099350)
XLA Ops:
  0.0 28.6 %fused.1 = f32[3,16,64]{2,1,0:T(8,128)S(1)} custom-call(f32[3,64]{1,0:T(4,128)} %pos_hbm.1, f32[3,16,64]{2,1,0:T(8,128)} %probes_hbm.1), custom_call_target="tpu_custom_call" | custom-call | tf_op jit(solution)/shard_map/fused/pallas_call | solution.py:284
  28.6 0.6 %copy.4 = f32[3,16,64]{2,1,0:T(8,128)} copy(f32[3,16,64]{2,1,0:T(8,128)S(1)} %fused.1) | data formatting | bytes 24576

commit v2 on v0

--- a/solution.py
+++ b/solution.py
@@ -21,11 +21,9 @@
     return 4.0 * (-1.0) ** (degree_step + 1) / (math.pi * (4.0 * degree_step * degree_step - 1.0))
 
 
-def flip(index, bits):
-    for bit in (1, 2, 4, 8):
-        if bits & bit:
-            index = index + bit - 2 * bit * lax.rem(lax.div(index, bit), 2)
-    return index
+def flips(index):
+    third = 3 - index
+    return [index, lax.rem(third + 2, 4), lax.rem(index + 2, 4), third]
 
 
 def split(value):
@@ -40,19 +38,20 @@
 ):
     row = lax.axis_index("row")
     col = lax.axis_index("col")
+    rows_by, cols_by = flips(row), flips(col)
     partners = [(dr, dc) for dc in range(4) for dr in (2, 3, 1, 0) if (dr, dc) != (0, 0)]
 
     loads = [
         pltpu.make_async_copy(pos_hbm, pos_ref, load.at[0]),
         pltpu.make_async_copy(probes_hbm, probes_ref, load.at[1]),
     ]
-    for copy in loads:
-        copy.start()
     barrier = pltpu.get_barrier_semaphore()
     for dr, dc in partners:
         pl.semaphore_signal(
-            barrier, inc=1, device_id={"row": flip(row, dr), "col": flip(col, dc)}, device_id_type=MESH
+            barrier, inc=1, device_id={"row": rows_by[dr], "col": cols_by[dc]}, device_id_type=MESH
         )
+    for copy in loads:
+        copy.start()
     for copy in loads:
         copy.wait()
 
@@ -60,20 +59,20 @@
     for r in range(4):
         mine = [probes_ref[t, 4 * r : 4 * r + 4, :] for t in range(3)]
         left = jnp.concatenate([mine[0], mine[1]], axis=0)
-        right = jnp.concatenate([mine[2], scaled_pos, jnp.zeros((1, 64), F32)], axis=0)
+        right = jnp.concatenate([mine[2], scaled_pos, jnp.ones((1, 64), F32)], axis=0)
         msg[r] = jnp.concatenate([left, right], axis=1)
     first[0, 0] = msg[row]
 
     pl.semaphore_wait(barrier, len(partners))
     first_copies = {}
     for dr, dc in partners:
-        to_row = flip(row, dr)
+        to_row = rows_by[dr]
         copy = pltpu.make_async_remote_copy(
             src_ref=msg.at[to_row],
             dst_ref=first.at[dc, dr],
             send_sem=first_send.at[dc, dr],
             recv_sem=first_recv.at[dc, dr],
-            device_id={"row": to_row, "col": flip(col, dc)},
+            device_id={"row": to_row, "col": cols_by[dc]},
             device_id_type=MESH,
         )
         copy.start()
@@ -96,12 +95,13 @@
     STEP = 16
     own_bead = lax.broadcasted_iota(jnp.int32, (STEP, 128), 1)
     step_bead = lax.broadcasted_iota(jnp.int32, (STEP, 128), 0)
-    sums = [[jnp.zeros((8, 128), F32) for _ in range(3)] for _ in range(2)]
-
-    def generate(dc, h):
+
+    def generate(dc, h, sums):
+        sums = [list(half) for half in sums]
         for at in range(0, 128, STEP):
             rows = slice(256 * dc + 128 * h + at, 256 * dc + 128 * h + at + STEP)
-            centres = [posT[dc, at : at + STEP, 8 * h + 4 + t : 8 * h + 5 + t] for t in range(3)]
+            centres = posT[dc, at : at + STEP, :]
+            centres = [centres[:, 8 * h + 4 + t : 8 * h + 5 + t] for t in range(3)]
             centres = [jnp.broadcast_to(c, (STEP, 128)) for c in centres]
             for own in range(2):
                 d = [field[0, 12 + t : 13 + t, 128 * own : 128 * own + 128] - centres[t] for t in range(3)]
@@ -128,96 +128,112 @@
                     lanes = slice(768 * own + 128 * k, 768 * own + 128 * k + 128)
                     w_high[rows, lanes] = high
                     w_low[rows, lanes] = low
-                mags = [jnp.abs(part) for part in parts]
-                mags = [mag[0:8] + mag[8:16] for mag in mags]
-                for t, (p, q, r) in enumerate(((0, 3, 4), (1, 3, 5), (2, 4, 5))):
-                    sums[own][t] = sums[own][t] + (mags[p] + mags[q] + mags[r])
+                for t in range(3):
+                    mag = jnp.abs(parts[3 + t])
+                    sums[own][t] = sums[own][t] + (mag[0:8] + mag[8:16])
+        return tuple(tuple(half) for half in sums)
 
     def multiply(blocks, dc):
         rows = slice(256 * dc, 256 * (dc + len(blocks)))
         high, low = split(jnp.concatenate(blocks, axis=1))
         both = jnp.concatenate([high, low], axis=0)
-        image = jnp.dot(both, w_high[rows], preferred_element_type=F32)
-        rest = jnp.dot(high, w_low[rows], preferred_element_type=F32)
+        image = jnp.dot(both, w_high[rows, :], preferred_element_type=F32)
+        rest = jnp.dot(high, w_low[rows, :], preferred_element_type=F32)
         return image[0:16] + image[16:32] + rest
 
     def combine(acc):
-        halves = []
-        for own in range(2):
-            xx, yy, zz, xy, xz, yz = [
-                acc[:, 768 * own + 128 * k : 768 * own + 128 * k + 128] for k in range(6)
-            ]
-            halves.append(
+        packed = []
+        at = {"x": (0, 3, 4), "y": (3, 1, 5), "z": (4, 5, 2)}
+        for component in "xyz":
+            for own in range(2):
+                terms = [
+                    acc[4 * t : 4 * t + 4, 768 * own + 128 * k : 768 * own + 128 * k + 128]
+                    for t, k in enumerate(at[component])
+                ]
+                packed.append(terms[0] + terms[1] + terms[2])
+        return jnp.concatenate(packed, axis=0)
+
+    def pack(block):
+        return jnp.concatenate(
+            [block[4 * t : 4 * t + 4, 128 * h : 128 * h + 128] for t in range(3) for h in range(2)], axis=0
+        )
+
+    def unpacked(packed):
+        return jnp.concatenate(
+            [
                 jnp.concatenate(
-                    [
-                        xx[0:4] + xy[4:8] + xz[8:12],
-                        xy[0:4] + yy[4:8] + yz[8:12],
-                        xz[0:4] + yz[4:8] + zz[8:12],
-                    ],
+                    [packed[8 * t + 4 * h : 8 * t + 4 * h + 4] for t in range(3)] + [jnp.zeros((4, 128), F32)],
                     axis=0,
                 )
-            )
-        return jnp.concatenate(halves, axis=1)
+                for h in range(2)
+            ],
+            axis=1,
+        )
+
+    gather_copies = {}
 
     def send(k, value):
-        gather[k, 0] = value
-        copies = {}
+        rows = slice(0, value.shape[0])
+        gather[k, 0, rows] = value
         for dc in (3, 2, 1):
-            copy = pltpu.make_async_remote_copy(
-                src_ref=gather.at[k, 0],
-                dst_ref=gather.at[k, dc],
+            gather_copies[k, dc] = pltpu.make_async_remote_copy(
+                src_ref=gather.at[k, 0, rows],
+                dst_ref=gather.at[k, dc, rows],
                 send_sem=gather_send.at[k, dc],
                 recv_sem=gather_recv.at[k, dc],
-                device_id={"row": row, "col": flip(col, dc)},
+                device_id={"row": row, "col": cols_by[dc]},
                 device_id_type=MESH,
             )
-            copy.start()
-            copies[dc] = copy
-        return copies
-
-    def apply(k, copies):
-        acc = multiply([gather[k, 0]], 0)
+            gather_copies[k, dc].start()
+
+    def apply(k):
+        acc = multiply([unpacked(gather[k, 0, 0:24])], 0)
         for dc in range(1, 4):
-            copies[dc].wait_recv()
-        return combine(acc + multiply([gather[k, dc] for dc in range(1, 4)], 1))
+            gather_copies[k, dc].wait_recv()
+        return combine(acc + multiply([unpacked(gather[k, dc, 0:24]) for dc in range(1, 4)], 1))
 
     for dr in (2, 3, 1):
         first_copies[0, dr].wait_recv()
     unpack(0)
-    generate(0, 0)
-    generate(0, 1)
+    sums = tuple(tuple(jnp.zeros((8, 128), F32) for _ in range(3)) for _ in range(2))
+    sums = generate(0, 0, sums)
+    sums = generate(0, 1, sums)
     for dc in range(1, 4):
         for dr in range(4):
             first_copies[dc, dr].wait_recv()
     for dc in range(1, 4):
         unpack(dc)
+
     acc = None
     for dc in range(1, 4):
-        generate(dc, 0)
+        sums = generate(dc, 0, sums)
         term = multiply([field[dc - 1]], dc - 1)
         acc = term if acc is None else acc + term
-        generate(dc, 1)
+        sums = generate(dc, 1, sums)
     acc = acc + multiply([field[3]], 3)
     image1 = combine(acc)
-    row_max = functools.reduce(jnp.maximum, [jnp.sum(s, axis=0, keepdims=True) for half in sums for s in half])
+    row_max = None
+    for own in range(2):
+        xx, yy, zz = [acc[15:16, 768 * own + 128 * k : 768 * own + 128 * k + 128] for k in range(3)]
+        xy, xz, yz = [jnp.sum(s, axis=0, keepdims=True) for s in sums[own]]
+        largest = jnp.maximum(jnp.maximum(xx + xy + xz, xy + yy + yz), xz + yz + zz)
+        row_max = largest if row_max is None else jnp.maximum(row_max, largest)
     row_max = jnp.max(row_max, axis=1, keepdims=True)
-    copies1 = send(0, jnp.concatenate([image1, jnp.broadcast_to(row_max, (4, 256))], axis=0))
-    image2 = apply(0, copies1)
-    top = functools.reduce(jnp.maximum, [gather[0, dc, 12:13, :] for dc in range(4)])
+    send(0, jnp.concatenate([image1, jnp.broadcast_to(row_max, (8, 128))], axis=0))
+    start = pack(field[0])
+    image2 = apply(0)
+    top = functools.reduce(jnp.maximum, [gather[0, dc, 24:25, :] for dc in range(4)])
     factor = 2.0 / top
-    start = field[0, 0:12, :]
     basis1 = factor * image1 - start
     basis2 = 2.0 * (factor * (factor * image2 - image1) - basis1) - start
-    pad = jnp.zeros((4, 256), F32)
-    copies2 = send(1, jnp.concatenate([basis2, pad], axis=0))
-    basis3 = 2.0 * (factor * apply(1, copies2) - basis2) - basis1
-    copies3 = send(2, jnp.concatenate([basis3, pad], axis=0))
-    noise = cheb_weight(0) * start + cheb_weight(1) * basis1
-    noise = noise + cheb_weight(2) * basis2 + cheb_weight(3) * basis3
-    basis4 = 2.0 * (factor * apply(2, copies3) - basis3) - basis2
-    noise = jnp.sqrt(top) * (noise + cheb_weight(4) * basis4)
-
-    noise = jnp.concatenate([noise, pad], axis=0)
+    send(1, basis2)
+    noise = cheb_weight(0) * start + cheb_weight(1) * basis1 + cheb_weight(2) * basis2
+    basis3 = 2.0 * (factor * apply(1) - basis2) - basis1
+    send(2, basis3)
+    noise = noise + cheb_weight(3) * basis3
+    basis4 = 2.0 * (factor * apply(2) - basis3) - basis2
+    noise = unpacked(jnp.sqrt(top) * (noise + cheb_weight(4) * basis4))
+
     last_copies = []
     for dr in (2, 3, 1, 0):
         h = dr // 2
@@ -236,16 +252,15 @@
                 dst_ref=last_in.at[row],
                 send_sem=last_send.at[dr],
                 recv_sem=last_recv.at[dr],
-                device_id={"row": flip(row, dr), "col": col},
+                device_id={"row": rows_by[dr], "col": col},
                 device_id_type=MESH,
             )
             copy.start()
             last_copies.append(copy)
     for copy in list(first_copies.values()):
         copy.wait_send()
-    for copies in (copies1, copies2, copies3):
-        for copy in copies.values():
-            copy.wait_send()
+    for copy in gather_copies.values():
+        copy.wait_send()
     for copy in last_copies:
         copy.wait()
     for q in range(4):
@@ -271,7 +286,7 @@
             pltpu.VMEM((4, 128, 16), F32),
             pltpu.VMEM((1024, 1536), BF16),
             pltpu.VMEM((1024, 1536), BF16),
-            pltpu.VMEM((DEG - 1, 4, 16, 256), F32),
+            pltpu.VMEM((DEG - 1, 4, 32, 128), F32),
             pltpu.VMEM((4, 8, 128), F32),
             pltpu.VMEM((4, 8, 128), F32),
             DMA((2,)),

time: 29.2 us -> 28.9 us (0.990)
  Pallas kernels: 28.4 us -> 28.1 us
where the time goes in v2:
time: 28.9 us; the launch traced here: 28.8 us
  Pallas kernels  28.1 us (97%)
  local copies, waits for them, and re-layouts  0.61 us (2%)
    pallas_call x1, Pallas kernels, fused(): pl.pallas_call(kernel, out_shape=jax.ShapeDtypeStruct(probes.shape, F32),...  28.1 us
    unnamed x1, local copies, waits for them, and re-layouts  0.61 us

profile of v2, /device:TPU:0, one launch (start us, length us, event | category | flops | bytes accessed | tf_op | source)
XLA Modules:
  0.0 28.8 jit_solution(10591247077845511858)
XLA Ops:
  0.0 28.1 %fused.1 = f32[3,16,64]{2,1,0:T(8,128)S(1)} custom-call(f32[3,64]{1,0:T(4,128)} %pos_hbm.1, f32[3,16,64]{2,1,0:T(8,128)} %probes_hbm.1), custom_call_target="tpu_custom_call" | custom-call | tf_op jit(solution)/shard_map/fused/pallas_call | solution.py:275
  28.2 0.6 %copy.4 = f32[3,16,64]{2,1,0:T(8,128)} copy(f32[3,16,64]{2,1,0:T(8,128)S(1)} %fused.1) | data formatting | bytes 24576

commit v3 on v2

--- a/solution.py
+++ b/solution.py
@@ -34,12 +34,12 @@
 def kernel(
     pos_hbm, probes_hbm, out_ref,
     pos_ref, probes_ref, msg, first, field, posT, w_high, w_low, gather, last_out, last_in,
-    load, first_send, first_recv, gather_send, gather_recv, last_send, last_recv,
+    load, row_send, row_recv, first_send, first_recv, gather_send, gather_recv, last_send, last_recv,
 ):
     row = lax.axis_index("row")
     col = lax.axis_index("col")
     rows_by, cols_by = flips(row), flips(col)
-    partners = [(dr, dc) for dc in range(4) for dr in (2, 3, 1, 0) if (dr, dc) != (0, 0)]
+    partners = [(2, 0), (3, 0), (1, 0), (0, 2), (0, 3), (0, 1)]
 
     loads = [
         pltpu.make_async_copy(pos_hbm, pos_ref, load.at[0]),
@@ -64,19 +64,17 @@
     first[0, 0] = msg[row]
 
     pl.semaphore_wait(barrier, len(partners))
-    first_copies = {}
-    for dr, dc in partners:
-        to_row = rows_by[dr]
-        copy = pltpu.make_async_remote_copy(
-            src_ref=msg.at[to_row],
-            dst_ref=first.at[dc, dr],
-            send_sem=first_send.at[dc, dr],
-            recv_sem=first_recv.at[dc, dr],
-            device_id={"row": to_row, "col": cols_by[dc]},
+    row_copies = {}
+    for dr in (2, 3, 1):
+        row_copies[dr] = pltpu.make_async_remote_copy(
+            src_ref=msg.at[rows_by[dr]],
+            dst_ref=first.at[0, dr],
+            send_sem=row_send.at[dr],
+            recv_sem=row_recv.at[dr],
+            device_id={"row": rows_by[dr], "col": col},
             device_id_type=MESH,
         )
-        copy.start()
-        first_copies[dc, dr] = copy
+        row_copies[dr].start()
 
     low_lanes = lax.broadcasted_iota(jnp.int32, (8, 128), 1) < 64
 
@@ -192,15 +190,25 @@
             gather_copies[k, dc].wait_recv()
         return combine(acc + multiply([unpacked(gather[k, dc, 0:24]) for dc in range(1, 4)], 1))
 
-    for dr in (2, 3, 1):
-        first_copies[0, dr].wait_recv()
+    for dr in (1, 2, 3):
+        row_copies[dr].wait_recv()
+    first_copies = {}
+    for dc in (2, 3, 1):
+        first_copies[dc] = pltpu.make_async_remote_copy(
+            src_ref=first.at[0],
+            dst_ref=first.at[dc],
+            send_sem=first_send.at[dc],
+            recv_sem=first_recv.at[dc],
+            device_id={"row": row, "col": cols_by[dc]},
+            device_id_type=MESH,
+        )
+        first_copies[dc].start()
     unpack(0)
     sums = tuple(tuple(jnp.zeros((8, 128), F32) for _ in range(3)) for _ in range(2))
     sums = generate(0, 0, sums)
     sums = generate(0, 1, sums)
     for dc in range(1, 4):
-        for dr in range(4):
-            first_copies[dc, dr].wait_recv()
+        first_copies[dc].wait_recv()
     for dc in range(1, 4):
         unpack(dc)
 
@@ -257,7 +265,7 @@
             )
             copy.start()
             last_copies.append(copy)
-    for copy in list(first_copies.values()):
+    for copy in [*row_copies.values(), *first_copies.values()]:
         copy.wait_send()
     for copy in gather_copies.values():
         copy.wait_send()
@@ -290,8 +298,10 @@
             pltpu.VMEM((4, 8, 128), F32),
             pltpu.VMEM((4, 8, 128), F32),
             DMA((2,)),
-            DMA((4, 4)),
-            DMA((4, 4)),
+            DMA((4,)),
+            DMA((4,)),
+            DMA((4,)),
+            DMA((4,)),
             DMA((DEG - 1, 4)),
             DMA((DEG - 1, 4)),
             DMA((4,)),

time: 28.9 us -> 29.9 us (1.035)
  Pallas kernels: 28.1 us -> 29.1 us
    pallas_call x1, Pallas kernels: 28.1 us -> 29.1 us  [fused(): pl.pallas_call(kernel, out_shape=jax.ShapeDtypeStruct(probes.shape, F32),...]
where the time goes in v3:
time: 29.9 us; the launch traced here: 29.7 us
  Pallas kernels  29.1 us (97%)
  local copies, waits for them, and re-layouts  0.61 us (2%)
    pallas_call x1, Pallas kernels, fused(): pl.pallas_call(kernel, out_shape=jax.ShapeDtypeStruct(probes.shape, F32),...  29.1 us
    unnamed x1, local copies, waits for them, and re-layouts  0.61 us

profile of v3, /device:TPU:0, one launch (start us, length us, event | category | flops | bytes accessed | tf_op | source)
XLA Modules:
  0.0 29.7 jit_solution(10758729543988362418)
XLA Ops:
  0.0 29.1 %fused.1 = f32[3,16,64]{2,1,0:T(8,128)S(1)} custom-call(f32[3,64]{1,0:T(4,128)} %pos_hbm.1, f32[3,16,64]{2,1,0:T(8,128)} %probes_hbm.1), custom_call_target="tpu_custom_call" | custom-call | tf_op jit(solution)/shard_map/fused/pallas_call | solution.py:283
  29.1 0.6 %copy.4 = f32[3,16,64]{2,1,0:T(8,128)} copy(f32[3,16,64]{2,1,0:T(8,128)S(1)} %fused.1) | data formatting | bytes 24576
